TPU v7x, 32 devices: a whole 2x2x4 slice. The times are simulated.
32 devices in a mesh: wa: 8 (over z, y), dev: 4 (over x, core).
Axes of the slice: x: 2, y: 2, z: 4, core: 2. Of those that a mesh axis runs over, the one named last changes fastest.
Arguments:
- output_gradient: bfloat16 [1024, 8192], P('wa'), may hold values from -6 to 6
- down_weight: bfloat16 [28672, 8192], P('dev', 'wa'), may hold values from -0.03125 to 0.03125
- gate_preactivation: bfloat16 [1024, 28672], P('wa', 'dev'), may hold values from -6 to 6
- up_preactivation: bfloat16 [1024, 28672], P('wa', 'dev'), may hold values from -6 to 6
- adapter_down_factor: bfloat16 [16, 16, 28672], P(None, None, 'dev'), may hold values from -0.0625 to 0.0625
- adapter_up_factor: bfloat16 [16, 16, 8192], P(None, None, 'dev'), may hold values from -0.0625 to 0.0625
- tile_owner_adapter: int32 [64, 1], replicated, may hold values from 0 to 15
- tile_live_count: int32 [64], replicated, may hold values from 1 to 16
Outputs:
- grad_gate: bfloat16 [1024, 28672], P('wa', 'dev')
- grad_up: bfloat16 [1024, 28672], P('wa', 'dev')
- grad_a: float32 [16, 16, 28672], P('wa', None, 'dev')
- grad_b: float32 [16, 16, 8192], P('wa', None, 'dev')
Inputs may be any that keep to these rules, and one draw needn't show every extreme that they name: `tile_owner_adapter`: every one of the 16 adapters owns at least one tile.
All inputs are finite; a program needn't handle non-finite values.
Results may differ from a plain program's by a relative error of at most 0.013.
Values may be sent and summed in bfloat16 or wider, within the bound.
No kernel may reach another device: no remote copies, remote signals or barrier semaphores. Data moves between devices by JAX's collectives and lax.ppermute only.
A program may use at most 128 MiB of HBM per device.

v0:
```python
import jax
import jax.numpy as jnp
from jax import lax
from jax.sharding import PartitionSpec as P

TILE = 16


def on_device(
    output_gradient,
    down_weight,
    gate_preactivation,
    up_preactivation,
    adapter_down_factor,
    adapter_up_factor,
    tile_owner_adapter,
    tile_live_count,
):
    wa_index = lax.axis_index("wa")
    dev_index = lax.axis_index("dev")
    token_rows = output_gradient.shape[0]
    hidden_local = down_weight.shape[0]
    shard_columns = adapter_up_factor.shape[2]
    adapter_list = adapter_down_factor.shape[0]
    adapter_rank_rows = adapter_down_factor.shape[1]
    tiles_local = token_rows // TILE
    own_adapter = lax.dynamic_slice_in_dim(
        tile_owner_adapter[:, 0], wa_index * tiles_local, tiles_local
    )
    own_live = lax.dynamic_slice_in_dim(tile_live_count, wa_index * tiles_local, tiles_local)
    row_adapter = jnp.repeat(own_adapter, TILE)
    position = jnp.arange(token_rows) % TILE
    live_rows = position < jnp.repeat(own_live, TILE)
    masked_rows = jnp.where(
        live_rows[:, None], output_gradient, jnp.zeros((), output_gradient.dtype)
    )
    gate_wide = gate_preactivation.astype(jnp.float32)
    up_wide = up_preactivation.astype(jnp.float32)
    hidden_state = (jax.nn.silu(gate_wide) * up_wide).astype(jnp.bfloat16)
    exchanged = lax.all_to_all(masked_rows, "wa", split_axis=1, concat_axis=0, tiled=True)
    base_grad = lax.psum_scatter(
        lax.dot_general(
            exchanged, down_weight, (((1,), (1,)), ((), ())), preferred_element_type=jnp.float32
        ).astype(jnp.bfloat16),
        "wa",
        scatter_dimension=0,
        tiled=True,
    ).astype(jnp.float32)
    selector = row_adapter[:, None] == jnp.arange(adapter_list, dtype=jnp.int32)[None, :]
    flattened_down = adapter_down_factor.reshape(adapter_list * adapter_rank_rows, hidden_local)
    flattened_up = adapter_up_factor.reshape(adapter_list * adapter_rank_rows, shard_columns)

    def choose_rows(complete_value):
        reshaped_value = complete_value.reshape(token_rows, adapter_list, adapter_rank_rows)
        return jnp.sum(
            jnp.where(selector[:, :, None], reshaped_value, jnp.zeros((), complete_value.dtype)),
            axis=1,
        )

    def spread_value(values):
        wide_value = jnp.where(
            selector[:, :, None], values[:, None, :], jnp.zeros((), values.dtype)
        )
        return wide_value.reshape(token_rows, adapter_list * adapter_rank_rows)

    grad_slice = lax.dynamic_slice_in_dim(masked_rows, dev_index * shard_columns, shard_columns, 1)
    in_partial = choose_rows(
        lax.dot_general(
            hidden_state,
            flattened_down,
            (((1,), (1,)), ((), ())),
            preferred_element_type=jnp.float32,
        )
    )
    out_partial = choose_rows(
        lax.dot_general(
            grad_slice, flattened_up, (((1,), (1,)), ((), ())), preferred_element_type=jnp.float32
        )
    )
    in_summed, out_summed = lax.psum((in_partial, out_partial), "dev")
    spread_input = spread_value(in_summed.astype(jnp.bfloat16))
    spread_output = spread_value(out_summed.astype(jnp.bfloat16))
    hidden_grad = base_grad + 2.0 * jnp.dot(
        spread_output, flattened_down, preferred_element_type=jnp.float32
    )
    sigmoid_gate = jax.nn.sigmoid(gate_wide)
    grad_up = (hidden_grad * gate_wide * sigmoid_gate).astype(jnp.bfloat16)
    grad_gate = (
        hidden_grad * up_wide * sigmoid_gate * (1.0 + gate_wide * (1.0 - sigmoid_gate))
    ).astype(jnp.bfloat16)
    down_factor_partial = 2.0 * lax.dot_general(
        spread_output, hidden_state, (((0,), (0,)), ((), ())), preferred_element_type=jnp.float32
    )
    up_factor_partial = 2.0 * lax.dot_general(
        spread_input, grad_slice, (((0,), (0,)), ((), ())), preferred_element_type=jnp.float32
    )
    down_factor_partial = down_factor_partial.reshape(adapter_list, adapter_rank_rows, hidden_local)
    up_factor_partial = up_factor_partial.reshape(adapter_list, adapter_rank_rows, shard_columns)
    grad_a, grad_b = (
        lax.psum_scatter(down_factor_partial, "wa", scatter_dimension=0, tiled=True),
        lax.psum_scatter(up_factor_partial, "wa", scatter_dimension=0, tiled=True),
    )
    return (grad_gate, grad_up, grad_a, grad_b)


def solution(mesh):
    placed = (
        P("wa", None),
        P("dev", "wa"),
        P("wa", "dev"),
        P("wa", "dev"),
        P(None, None, "dev"),
        P(None, None, "dev"),
        P(),
        P(),
    )
    return jax.shard_map(
        on_device,
        mesh=mesh,
        in_specs=placed,
        out_specs=(P("wa", "dev"), P("wa", "dev"), P("wa", None, "dev"), P("wa", None, "dev")),
        check_vma=False,
    )
```

profile of v0, /device:TPU:0, one launch (start us, length us, event | category | flops | bytes accessed | tf_op | source)
XLA Modules:
  0.0 537.0 jit_solution(9051864662118569720)
XLA Ops:
  7.2 0.0 copy-start
  7.2 0.0 reduce-scatter.4.cloned.1.call-start
  7.2 0.8 dynamic_slice.11
  8.0 0.1 broadcast_in_dim.69
  8.1 0.1 reshape.79
  8.2 1.8 broadcast_select_fusion
  10.0 0.2 copy.15
  10.2 55.4 %all_to_all.19 = bf16[128,8,1024]{2,0,1:T(8,128)(2,1)} all-to-all(bf16[128,8,1024]{2,0,1:T(8,128)(2,1)S(1)} %bitcast.38), channel_id=1, replica_groups=mesh['wa'=8,'dev'=4] {'wa'}, dimensions={1} | all-to-all | bytes 4194304 | tf_op jit(solution)/shard_map/all_to_all | solution.py:40
  65.6 22.3 %convolution_convert_fusion = bf16[1024,7168]{1,0:T(8,128)(2,1)} fusion(bf16[1024,1024]{1,0:T(8,128)(2,1)} %bitcast.40, bf16[7168,1024]{1,0:T(8,128)(2,1)} %param.9), kind=kOutput, calls=%fused_computation | convolution fusion | flops 15039725568 | bytes 31457280 | tf_op jit(solution)/shard_map/dot_general | solution.py:42
  88.0 0.0 copy-start.2
  88.0 0.0 reduce-scatter.4.cloned.1.call-update
  88.0 0.0 reduce-scatter.8.cloned.1.call-start
  88.0 0.6 copy-done.2
  88.6 0.1 dynamic-slice_bitcast_fusion
  88.7 0.1 broadcast_in_dim.72
  88.8 0.1 eq.21
  88.9 0.0 copy-done
  88.9 0.4 fusion.20
  89.3 4.8 fusion.17
  94.1 11.0 %all-reduce = (bf16[128,16]{0,1:T(8,128)(2,1)S(1)}, bf16[128,16]{0,1:T(8,128)(2,1)S(1)}) all-reduce(f32[128,16]{0,1:T(8,128)S(1)} %fusion.20, f32[128,16]{0,1:T(8,128)S(1)} %fusion.17), channel_id=1, replica_groups=mesh['wa'=8,'dev'=4] {'dev'}, use_global_device_ids=true, to_apply=%region_2.3 | all-reduce | flops 4096 | bytes 24576 | tf_op jit(solution)/shard_map/psum | solution.py:80
  105.1 1.8 convolution_multiply_fusion.1
  106.9 0.0 reduce-scatter.8.cloned.1.call-update
  106.9 0.2 reduce-scatter.6.cloned.1.call-start
  107.1 6.8 %convolution_multiply_fusion = f32[256,7168]{1,0:T(8,128)} fusion(bf16[128,256]{0,1:T(8,128)(2,1)S(1)} %bitcast.42, bf16[128,7168]{1,0:T(8,128)(2,1)} %param.11, bf16[128,7168]{1,0:T(8,128)(2,1)} %param.10), kind=kOutput, calls=%fused_computation.1 | convolution fusion | flops 478937088 | bytes 11075584 | tf_op jit(solution)/shard_map/dot_general | solution.py:91
  114.0 0.0 copy-start.1
  114.0 0.0 reduce-scatter.6.cloned.1.call-update
  114.0 209.7 %reduce-scatter.4.cloned.1.call-done = bf16[128,7168]{1,0:T(8,128)(2,1)} async-done(((bf16[1024,7168]{1,0:T(8,128)(2,1)}), bf16[128,7168]{1,0:T(8,128)(2,1)}) %reduce-scatter.4.cloned.1.call-update) | async-done | bytes 1835024 | tf_op jit(solution)/shard_map/reduce_scatter | solution.py:41
  323.7 0.0 copy-done.1
  323.7 7.6 %fusion.11 = (bf16[128,7168]{1,0:T(8,128)(2,1)}, bf16[128,7168]{1,0:T(8,128)(2,1)}) fusion(bf16[128,7168]{1,0:T(8,128)(2,1)S(1)} %copy-done.1, bf16[128,7168]{1,0:T(8,128)(2,1)} %param.11, bf16[16,16,7168]{2,1,0:T(8,128)(2,1)} %param.12, pred[128,16]{0,1:T(8,128)(4,1)S(1)} %iota_compare_fusion, bf16[128,16]{0,1:T(8,128)(2,1)S(1)} %get-tuple-element.4, ...), kind=kOutput, calls=%fused_computation.20 | convolution fusion | flops 486309888 | bytes 12851200 | tf_op jit(solution)/shard_map/dot_general | solution.py:83
  331.3 63.3 %reduce-scatter.8.cloned.1.call-done = f32[2,16,2048]{2,1,0:T(8,128)} async-done(((f32[16,16,2048]{2,1,0:T(8,128)}), f32[2,16,2048]{2,1,0:T(8,128)}) %reduce-scatter.8.cloned.1.call-update) | async-done | bytes 262160 | tf_op jit(solution)/shard_map/reduce_scatter | solution.py:101
  394.5 135.9 %reduce-scatter.6.cloned.1.call-done = f32[2,16,7168]{2,1,0:T(8,128)} async-done(((f32[16,16,7168]{2,1,0:T(8,128)}), f32[2,16,7168]{2,1,0:T(8,128)}) %reduce-scatter.6.cloned.1.call-update) | async-done | bytes 917520 | tf_op jit(solution)/shard_map/reduce_scatter | solution.py:100
  (3 shorter events, 0.0 us)
Async XLA Ops:
  7.2 81.7 %copy-start = (bf16[16,16,2048]{2,1,0:T(8,128)(2,1)S(1)}, bf16[16,16,2048]{2,1,0:T(8,128)(2,1)}, u32[]{:S(2)}) copy-start(bf16[16,16,2048]{2,1,0:T(8,128)(2,1)} %param.13) | copy-start | bytes 3145732
  7.2 316.5 %reduce-scatter.4.cloned.1.call-start = ((), (), s32[]{:S(2)}) async-start(), calls=%async_computation.4 | async-start | bytes 16515072 | tf_op jit(solution)/shard_map/reduce_scatter | solution.py:41
  88.0 0.7 copy-start.2
  88.0 306.5 %reduce-scatter.8.cloned.1.call-start = ((), (), s32[]{:S(2)}) async-start(), calls=%async_computation.6 | async-start | bytes 2359296 | tf_op jit(solution)/shard_map/reduce_scatter | solution.py:101
  106.9 423.5 %reduce-scatter.6.cloned.1.call-start = ((), (), s32[]{:S(2)}) async-start(), calls=%async_computation.5 | async-start | bytes 8257536 | tf_op jit(solution)/shard_map/reduce_scatter | solution.py:100
  114.0 209.7 %copy-start.1 = (bf16[128,7168]{1,0:T(8,128)(2,1)S(1)}, bf16[128,7168]{1,0:T(8,128)(2,1)}, u32[]{:S(2)}) copy-start(bf16[128,7168]{1,0:T(8,128)(2,1)} %param.10) | copy-start | bytes 5505028
Sparse Core Ops, SparseCore 0:
  88.1 235.4 reduce-scatter.3
  327.8 66.7 reduce-scatter.7
  398.7 131.6 reduce-scatter.5
where the time goes:
time: 537 us
  waiting for transfers between devices  409 us (76%)
  blocking collectives  66.4 us (12%)
  matrix products  43.8 us (8%)
  between operations  13.8 us (3%)
    reduce_scatter x1, waiting for transfers between devices, on_device(): lax.psum_scatter(lax.dot_general(exchanged, down_weight, (((1,), (1,)), (...  210 us
    reduce_scatter x1, waiting for transfers between devices, on_device(): lax.psum_scatter(down_factor_partial, 'wa', scatter_dimension=0, tiled=True)  136 us
    reduce_scatter x1, waiting for transfers between devices, on_device(): lax.psum_scatter(up_factor_partial, 'wa', scatter_dimension=0, tiled=True)  63.3 us
    all_to_all x1, blocking collectives, on_device(): lax.all_to_all(masked_rows, 'wa', split_axis=1, concat_axis=0, tiled=True)  55.4 us
    dot_general x1, matrix products, on_device(): lax.dot_general(exchanged, down_weight, (((1,), (1,)), ((), ())), preferr...  22.3 us
    psum x1, blocking collectives, on_device(): in_summed, out_summed = lax.psum((in_partial, out_partial), 'dev')  11 us
  transfers between devices with their start and end apart: 3, of which 3 were waited for; matrix products, arithmetic and copies ran while one was open for 4% of the time, Pallas kernels for 0%

commit v1 on v0

v1 whole, which is shorter than its diff:
```python
import jax
import jax.numpy as jnp
from jax import lax
from jax.sharding import PartitionSpec as P

TILE = 16
BF16 = jnp.bfloat16
F32 = jnp.float32


def nt_dot(left, right):
    return lax.dot_general(left, right, (((1,), (1,)), ((), ())), preferred_element_type=F32)


def tn_dot(left, right):
    return lax.dot_general(left, right, (((0,), (0,)), ((), ())), preferred_element_type=F32)


def ring_order(length):
    return [0] + list(range(1, length, 2)) + [z for z in range(length - 1, 0, -1) if z % 2 == 0]


class Group:
    def __init__(self, size):
        self.size = size
        self.length = size // 2
        self.order = ring_order(self.length)
        self.places = [(place, half) for place in range(self.length) for half in range(2)]

    def rank(self, place, half):
        return self.order[place % self.length] * 2 + half

    def swap_pairs(self):
        return [(w, w ^ 1) for w in range(self.size)]

    def next_pairs(self):
        return [(self.rank(p, h), self.rank(p + 1, h)) for p, h in self.places]

    def fetch_pairs(self, ahead, flip):
        return [(self.rank(p + ahead, h ^ flip), self.rank(p, h)) for p, h in self.places]

    def table(self, ahead, flip):
        entries = [0] * self.size
        for p, h in self.places:
            entries[self.rank(p, h)] = self.rank(p + ahead, h ^ flip)
        return entries


def add_round(first, second):
    return (first.astype(F32) + second.astype(F32)).astype(BF16)


def ring_sum(group, parts):
    travelling = parts[-1]
    for part in parts[-2::-1]:
        arrived = lax.ppermute(travelling, "wa", group.next_pairs())
        total = part.astype(F32) + arrived.astype(F32)
        travelling = total.astype(BF16)
    return total


def butterfly_sum(value, count):
    step = count // 2
    while step:
        value = value + lax.ppermute(value, "dev", [(d, d ^ step) for d in range(count)])
        step //= 2
    return value


def butterfly_gather(block, count):
    held = block[None]
    spans = [0]
    step = count // 2
    while step:
        other = lax.ppermute(held, "dev", [(d, d ^ step) for d in range(count)])
        held = jnp.concatenate([held, other], axis=0)
        spans = spans + [s ^ step for s in spans]
        step //= 2
    return [held[spans.index(j)] for j in range(count)], held, spans


def chunk_count(columns):
    for count in (7, 8, 4, 2):
        if columns % (128 * count) == 0:
            return count
    return 1


def run(
    rows,
    wa_size,
    dev_size,
    output_gradient,
    down_weight,
    gate_preactivation,
    up_preactivation,
    adapter_down_factor,
    adapter_up_factor,
    tile_owner_adapter,
    tile_live_count,
):
    group = Group(wa_size)
    length = group.length
    me = lax.axis_index("wa")
    dev = lax.axis_index("dev")
    token_rows, model_width = output_gradient.shape
    hidden_local = down_weight.shape[0]
    group_width = down_weight.shape[1]
    shard_columns = adapter_up_factor.shape[2]
    adapters, rank = adapter_down_factor.shape[:2]
    owned = adapters // wa_size
    tiles = token_rows // TILE
    sub_width = group_width // dev_size

    own_adapter = lax.dynamic_slice_in_dim(tile_owner_adapter[:, 0], me * tiles, tiles)
    own_live = lax.dynamic_slice_in_dim(tile_live_count, me * tiles, tiles)
    begin = jnp.cumsum(own_live) - own_live
    position = jnp.arange(token_rows, dtype=jnp.int32) % TILE
    target = jnp.where(
        position < jnp.repeat(own_live, TILE), jnp.repeat(begin, TILE) + position, -1
    )
    pick = (jnp.arange(rows, dtype=jnp.int32)[:, None] == target[None, :]).astype(BF16)
    row_adapter = jnp.repeat(own_adapter, TILE)

    def compact(values):
        return jnp.dot(pick, values, preferred_element_type=F32).astype(BF16)

    pieces = []
    for flip in (1, 0):
        for ahead in range(length):
            target_device = jnp.array(group.table(-ahead, flip), jnp.int32)[me]
            piece = compact(
                lax.dynamic_slice_in_dim(
                    output_gradient, target_device * group_width + dev * sub_width, sub_width, 1
                )
            )
            if flip or ahead:
                piece = lax.ppermute(piece, "wa", group.fetch_pairs(ahead, flip))
            pieces.append(piece)
    mine = jnp.concatenate(pieces, axis=0)
    _, held, spans = butterfly_gather(mine, dev_size)
    place_of = jnp.array([spans.index(j) for j in range(dev_size)], jnp.int32)
    columns = jnp.concatenate(
        [
            lax.dynamic_index_in_dim(held, place_of[jnp.bitwise_xor(dev, j)], 0, keepdims=False)
            for j in range(dev_size)
        ],
        axis=1,
    )
    columns_other = columns[: length * rows]
    columns_own = columns[length * rows :]

    flat_down = adapter_down_factor.reshape(adapters * rank, hidden_local)
    flat_up = adapter_up_factor.reshape(adapters * rank, shard_columns)
    grad_slice = compact(
        lax.dynamic_slice_in_dim(output_gradient, dev * shard_columns, shard_columns, 1)
    )
    gate = compact(gate_preactivation).astype(F32)
    up = compact(up_preactivation).astype(F32)
    hidden = (jax.nn.silu(gate) * up).astype(BF16)

    def selector_for(order):
        return jnp.dot(
            pick, (row_adapter[:, None] == order[None, :]).astype(BF16), preferred_element_type=F32
        )

    adapter_order = jnp.arange(adapters, dtype=jnp.int32)
    selector = selector_for(adapter_order)
    owners = jnp.array(
        [group.table(ahead, flip) for ahead in range(length) for flip in (1, 0)], jnp.int32
    )[:, me]
    owner_order = (owners[:, None] * owned + jnp.arange(owned, dtype=jnp.int32)).reshape(adapters)
    owner_selector = selector_for(owner_order)

    def choose(values):
        return jnp.sum(
            values.reshape(rows, adapters, rank) * selector[:, :, None], axis=1
        )

    def spread(values, which):
        wide = values[:, None, :] * which.astype(BF16)[:, :, None]
        return wide.reshape(rows, adapters * rank)

    lora = jnp.concatenate(
        [choose(nt_dot(hidden, flat_down)), choose(nt_dot(grad_slice, flat_up))], axis=1
    )
    lora = butterfly_sum(lora, dev_size).astype(BF16)
    lora_in, lora_out = lora[:, :rank], lora[:, rank:]
    spread_out = spread(lora_out, selector)

    def owner_sum(lora_values, values):
        partial = tn_dot(spread(lora_values, owner_selector), values).astype(BF16)
        partial = partial.reshape(length, 2, owned * rank, values.shape[1])
        both = ring_sum(group, [partial[k] for k in range(length)])
        arrived = lax.ppermute(both[0].astype(BF16), "wa", group.swap_pairs())
        total = 2.0 * (both[1] + arrived.astype(F32))
        return total.reshape(owned, rank, values.shape[1])

    grad_a = owner_sum(lora_out, hidden)
    grad_b = owner_sum(lora_in, grad_slice)

    chunks = chunk_count(hidden_local)
    width = hidden_local // chunks
    grad_gate_parts, grad_up_parts = [], []
    for chunk in range(chunks):
        span = slice(chunk * width, (chunk + 1) * width)
        weights = down_weight[span]
        away = nt_dot(columns_other, weights).astype(BF16)
        arrived = lax.ppermute(away, "wa", group.swap_pairs())
        paired = add_round(nt_dot(columns_own, weights), arrived)
        base = ring_sum(group, [paired[k * rows : (k + 1) * rows] for k in range(length)])
        hidden_grad = base + 2.0 * jnp.dot(
            spread_out, flat_down[:, span], preferred_element_type=F32
        )
        gate_here, up_here = gate[:, span], up[:, span]
        sigmoid = jax.nn.sigmoid(gate_here)
        grad_up = (hidden_grad * gate_here * sigmoid).astype(BF16)
        grad_gate = (
            hidden_grad * up_here * sigmoid * (1.0 + gate_here * (1.0 - sigmoid))
        ).astype(BF16)
        grad_up_parts.append(tn_dot(pick, grad_up).astype(BF16))
        grad_gate_parts.append(tn_dot(pick, grad_gate).astype(BF16))
    return (
        jnp.concatenate(grad_gate_parts, axis=1),
        jnp.concatenate(grad_up_parts, axis=1),
        grad_a,
        grad_b,
    )


def solution(mesh):
    wa_size, dev_size = mesh.shape["wa"], mesh.shape["dev"]

    def on_device(output_gradient, *others):
        return run(output_gradient.shape[0], wa_size, dev_size, output_gradient, *others)

    placed = (
        P("wa", None),
        P("dev", "wa"),
        P("wa", "dev"),
        P("wa", "dev"),
        P(None, None, "dev"),
        P(None, None, "dev"),
        P(),
        P(),
    )
    return jax.shard_map(
        on_device,
        mesh=mesh,
        in_specs=placed,
        out_specs=(P("wa", "dev"), P("wa", "dev"), P("wa", None, "dev"), P("wa", None, "dev")),
        check_vma=False,
    )
```

time: 537 us -> 395 us (0.74)
  waiting for transfers between devices: 409 us -> 257 us
  blocking collectives: 66.4 us -> 0 us
  starting transfers between devices: 0.3 us -> 54.3 us
  local copies, waits for them, and re-layouts: 1.95 us -> 12.5 us
  matrix products: 43.8 us -> 50.8 us
    reduce_scatter x3 -> x0, waiting for transfers between devices: 409 us -> none  [the longest x1 210 us: on_device(): lax.psum_scatter(lax.dot_general(exchanged, down_weight, (((1,), (1,)), (...]
    ppermute x0 -> x47, waiting for transfers between devices: none -> 257 us  [the longest x7 130 us: run(): arrived = lax.ppermute(away, 'wa', group.swap_pairs())]
    all_to_all x1 -> x0, blocking collectives: 55.4 us -> none  [on_device(): lax.all_to_all(masked_rows, 'wa', split_axis=1, concat_axis=0, tiled=True)]
    ppermute x0 -> x47, starting transfers between devices: none -> 54.3 us  [the longest x27 25.7 us: ring_sum(): arrived = lax.ppermute(travelling, 'wa', group.next_pairs())]
    psum x1 -> x0, blocking collectives: 11 us -> none  [on_device(): in_summed, out_summed = lax.psum((in_partial, out_partial), 'dev')]
    dot_general x6 -> x52, matrix products: 43.8 us -> 50.8 us  [the longest x16 22.2 us: nt_dot(): lax.dot_general(left, right, (((1,), (1,)), ((), ())), preferred_element_...]
  transfers between devices with their start and end apart: 3 -> 47, of which waited for: 3 -> 31; matrix products, arithmetic and copies ran while one was open for 4% -> 12% of each run, Pallas kernels for 0% -> 0%
where the time goes in v1:
time: 395 us; the launch traced here: 394 us
  waiting for transfers between devices  257 us (65%)
  starting transfers between devices  54.3 us (14%)
  matrix products  50.8 us (13%)
  between operations  13.9 us (4%)
  local copies, waits for them, and re-layouts  12.5 us (3%)
  other arithmetic  5.78 us (1%)
    ppermute x7, waiting for transfers between devices, run(): arrived = lax.ppermute(away, 'wa', group.swap_pairs())  130 us
    ppermute x27, waiting for transfers between devices, ring_sum(): arrived = lax.ppermute(travelling, 'wa', group.next_pairs())  124 us
    ppermute x27, starting transfers between devices, ring_sum(): arrived = lax.ppermute(travelling, 'wa', group.next_pairs())  25.7 us
    dot_general x16, matrix products, nt_dot(): lax.dot_general(left, right, (((1,), (1,)), ((), ())), preferred_element_...  22.2 us
    ppermute x7, starting transfers between devices, run(): piece = lax.ppermute(piece, 'wa', group.fetch_pairs(ahead, flip))  13 us
    dot_general x11, matrix products, compact(): return jnp.dot(pick, values, preferred_element_type=F32).astype(BF16)  11.7 us
    dot_general x7, matrix products, run(): jnp.dot(spread_out, flat_down[:, span], preferred_element_type=F32)  9.23 us
    ppermute x7, starting transfers between devices, run(): arrived = lax.ppermute(away, 'wa', group.swap_pairs())  8.69 us
  transfers between devices with their start and end apart: 47, of which 31 were waited for; matrix products, arithmetic and copies ran while one was open for 12% of the time, Pallas kernels for 0%

profile of v1, /device:TPU:0, one launch (start us, length us, event | category | flops | bytes accessed | tf_op | source)
XLA Modules:
  0.0 393.8 jit_solution(11038111102006646276)
XLA Ops:
  4.4 3.9 fusion.1
  8.5 6.2 %multiply_convert_fusion = (bf16[128,7168]{1,0:T(8,128)(2,1)}, f32[128,7168]{1,0:T(8,128)}) fusion(f32[128,7168]{1,0:T(8,128)} %fusion.1, bf16[128,7168]{1,0:T(8,128)(2,1)} %param.21, s32[128]{0:T(128)S(1)} %compare_select_fusion), kind=kOutput, calls=%fused_computation.5 | convolution fusion | flops 242237440 | bytes 11010560 | tf_op jit(solution)/shard_map/dot_general | solution.py:126
  15.1 3.8 fusion.87
  19.4 3.0 collective-permute-start.13
  23.8 1.6 collective-permute-start
  26.8 2.6 collective-permute-start.1
  30.8 2.4 collective-permute-start.2
  49.2 2.2 collective-permute-start.4
  51.4 1.3 convolution_multiply_fusion.6
  52.7 1.3 convolution_multiply_fusion.5
  54.0 1.3 convolution_multiply_fusion.4
  55.3 1.3 convolution_multiply_fusion.3
  56.6 1.3 convolution_multiply_fusion.2
  57.9 1.3 convolution_multiply_fusion.1
  62.1 1.5 convolution_multiply_fusion
  63.8 2.4 collective-permute-start.5
  67.3 7.8 %collective-permute-done.43 = bf16[2,32,2048]{2,1,0:T(8,128)(2,1)S(1)} collective-permute-done((bf16[2,32,2048]{2,1,0:T(8,128)(2,1)S(1)}, bf16[2,32,2048]{2,1,0:T(8,128)(2,1)S(1)}, u32[]{:S(2)}, u32[]{:S(2)}) %collective-permute-start.43) | collective-permute-done | bytes 262176 | tf_op jit(solution)/shard_map/ppermute | solution.py:56
  75.2 3.1 collective-permute-start.44
  78.4 24.1 %collective-permute-done.44 = bf16[2,32,2048]{2,1,0:T(8,128)(2,1)S(1)} collective-permute-done((bf16[2,32,2048]{2,1,0:T(8,128)(2,1)S(1)}, bf16[2,32,2048]{2,1,0:T(8,128)(2,1)S(1)}, u32[]{:S(2)}, u32[]{:S(2)}) %collective-permute-start.44) | collective-permute-done | bytes 262176 | tf_op jit(solution)/shard_map/ppermute | solution.py:56
  103.3 6.6 %collective-permute-done.45 = bf16[2,32,2048]{2,1,0:T(8,128)(2,1)S(1)} collective-permute-done((bf16[2,32,2048]{2,1,0:T(8,128)(2,1)S(1)}, bf16[2,32,2048]{2,1,0:T(8,128)(2,1)S(1)}, u32[]{:S(2)}, u32[]{:S(2)}) %collective-permute-start.45) | collective-permute-done | bytes 262176 | tf_op jit(solution)/shard_map/ppermute | solution.py:56
  110.0 1.6 collective-permute-start.46
  111.5 2.7 collective-permute-done.7
  115.9 2.6 collective-permute-start.40
  119.2 1.7 slice-done.3
  127.4 1.6 collective-permute-start.9
  129.5 1.5 collective-permute-start.19
  134.1 5.2 %collective-permute-done.40 = bf16[2,32,7168]{2,1,0:T(8,128)(2,1)S(1)} collective-permute-done((bf16[2,32,7168]{2,1,0:T(8,128)(2,1)S(1)}, bf16[2,32,7168]{2,1,0:T(8,128)(2,1)S(1)}, u32[]{:S(2)}, u32[]{:S(2)}) %collective-permute-start.40) | collective-permute-done | bytes 917536 | tf_op jit(solution)/shard_map/ppermute | solution.py:56
  139.3 1.5 collective-permute-start.27
  141.0 12.4 %collective-permute-done.9 = bf16[512,1024]{1,0:T(8,128)(2,1)S(1)} collective-permute-done((bf16[512,1024]{1,0:T(8,128)(2,1)S(1)}, bf16[512,1024]{1,0:T(8,128)(2,1)S(1)}, u32[]{:S(2)}, u32[]{:S(2)}) %collective-permute-start.9) | collective-permute-done | bytes 1048608 | tf_op jit(solution)/shard_map/ppermute | solution.py:209
  153.4 1.5 collective-permute-start.31
  156.3 19.7 %collective-permute-done.15 = bf16[512,1024]{1,0:T(8,128)(2,1)S(1)} collective-permute-done((bf16[512,1024]{1,0:T(8,128)(2,1)S(1)}, bf16[512,1024]{1,0:T(8,128)(2,1)S(1)}, u32[]{:S(2)}, u32[]{:S(2)}) %collective-permute-start.15) | collective-permute-done | bytes 1048608 | tf_op jit(solution)/shard_map/ppermute | solution.py:209
  175.9 1.5 collective-permute-start.35
  178.7 19.7 %collective-permute-done.19 = bf16[512,1024]{1,0:T(8,128)(2,1)S(1)} collective-permute-done((bf16[512,1024]{1,0:T(8,128)(2,1)S(1)}, bf16[512,1024]{1,0:T(8,128)(2,1)S(1)}, u32[]{:S(2)}, u32[]{:S(2)}) %collective-permute-start.19) | collective-permute-done | bytes 1048608 | tf_op jit(solution)/shard_map/ppermute | solution.py:209
  198.4 1.5 collective-permute-start.41
  201.2 19.7 %collective-permute-done.23 = bf16[512,1024]{1,0:T(8,128)(2,1)S(1)} collective-permute-done((bf16[512,1024]{1,0:T(8,128)(2,1)S(1)}, bf16[512,1024]{1,0:T(8,128)(2,1)S(1)}, u32[]{:S(2)}, u32[]{:S(2)}) %collective-permute-start.23) | collective-permute-done | bytes 1048608 | tf_op jit(solution)/shard_map/ppermute | solution.py:209
  220.9 1.5 collective-permute-start.10
  223.6 19.7 %collective-permute-done.27 = bf16[512,1024]{1,0:T(8,128)(2,1)S(1)} collective-permute-done((bf16[512,1024]{1,0:T(8,128)(2,1)S(1)}, bf16[512,1024]{1,0:T(8,128)(2,1)S(1)}, u32[]{:S(2)}, u32[]{:S(2)}) %collective-permute-start.27) | collective-permute-done | bytes 1048608 | tf_op jit(solution)/shard_map/ppermute | solution.py:209
  243.3 1.5 collective-permute-start.16
  246.2 19.6 %collective-permute-done.31 = bf16[512,1024]{1,0:T(8,128)(2,1)S(1)} collective-permute-done((bf16[512,1024]{1,0:T(8,128)(2,1)S(1)}, bf16[512,1024]{1,0:T(8,128)(2,1)S(1)}, u32[]{:S(2)}, u32[]{:S(2)}) %collective-permute-start.31) | collective-permute-done | bytes 1048608 | tf_op jit(solution)/shard_map/ppermute | solution.py:209
  265.8 1.5 collective-permute-start.20
  268.6 19.0 %collective-permute-done.35 = bf16[512,1024]{1,0:T(8,128)(2,1)S(1)} collective-permute-done((bf16[512,1024]{1,0:T(8,128)(2,1)S(1)}, bf16[512,1024]{1,0:T(8,128)(2,1)S(1)}, u32[]{:S(2)}, u32[]{:S(2)}) %collective-permute-start.35) | collective-permute-done | bytes 1048608 | tf_op jit(solution)/shard_map/ppermute | solution.py:209
  287.6 1.5 collective-permute-start.24
  291.0 1.4 collective-permute-start.32
  292.6 1.8 collective-permute-start.36
  294.4 1.6 collective-permute-start.42
  296.1 1.6 collective-permute-done.24
  298.3 5.0 %collective-permute-done.28 = bf16[128,1024]{1,0:T(8,128)(2,1)S(1)} collective-permute-done((bf16[128,1024]{1,0:T(8,128)(2,1)S(1)}, bf16[128,1024]{1,0:T(8,128)(2,1)S(1)}, u32[]{:S(2)}, u32[]{:S(2)}) %collective-permute-start.28) | collective-permute-done | bytes 262176 | tf_op jit(solution)/shard_map/ppermute | solution.py:56
  304.0 5.0 %collective-permute-done.32 = bf16[128,1024]{1,0:T(8,128)(2,1)S(1)} collective-permute-done((bf16[128,1024]{1,0:T(8,128)(2,1)S(1)}, bf16[128,1024]{1,0:T(8,128)(2,1)S(1)}, u32[]{:S(2)}, u32[]{:S(2)}) %collective-permute-start.32) | collective-permute-done | bytes 262176 | tf_op jit(solution)/shard_map/ppermute | solution.py:56
  309.6 5.0 %collective-permute-done.36 = bf16[128,1024]{1,0:T(8,128)(2,1)S(1)} collective-permute-done((bf16[128,1024]{1,0:T(8,128)(2,1)S(1)}, bf16[128,1024]{1,0:T(8,128)(2,1)S(1)}, u32[]{:S(2)}, u32[]{:S(2)}) %collective-permute-start.36) | collective-permute-done | bytes 262176 | tf_op jit(solution)/shard_map/ppermute | solution.py:56
  315.2 5.0 %collective-permute-done.11 = bf16[128,1024]{1,0:T(8,128)(2,1)S(1)} collective-permute-done((bf16[128,1024]{1,0:T(8,128)(2,1)S(1)}, bf16[128,1024]{1,0:T(8,128)(2,1)S(1)}, u32[]{:S(2)}, u32[]{:S(2)}) %collective-permute-start.11) | collective-permute-done | bytes 262176 | tf_op jit(solution)/shard_map/ppermute | solution.py:56
  320.8 5.0 %collective-permute-done.17 = bf16[128,1024]{1,0:T(8,128)(2,1)S(1)} collective-permute-done((bf16[128,1024]{1,0:T(8,128)(2,1)S(1)}, bf16[128,1024]{1,0:T(8,128)(2,1)S(1)}, u32[]{:S(2)}, u32[]{:S(2)}) %collective-permute-start.17) | collective-permute-done | bytes 262176 | tf_op jit(solution)/shard_map/ppermute | solution.py:56
  326.4 5.0 %collective-permute-done.21 = bf16[128,1024]{1,0:T(8,128)(2,1)S(1)} collective-permute-done((bf16[128,1024]{1,0:T(8,128)(2,1)S(1)}, bf16[128,1024]{1,0:T(8,128)(2,1)S(1)}, u32[]{:S(2)}, u32[]{:S(2)}) %collective-permute-start.21) | collective-permute-done | bytes 262176 | tf_op jit(solution)/shard_map/ppermute | solution.py:56
  332.1 5.0 %collective-permute-done.25 = bf16[128,1024]{1,0:T(8,128)(2,1)S(1)} collective-permute-done((bf16[128,1024]{1,0:T(8,128)(2,1)S(1)}, bf16[128,1024]{1,0:T(8,128)(2,1)S(1)}, u32[]{:S(2)}, u32[]{:S(2)}) %collective-permute-start.25) | collective-permute-done | bytes 262176 | tf_op jit(solution)/shard_map/ppermute | solution.py:56
  337.7 5.0 %collective-permute-done.29 = bf16[128,1024]{1,0:T(8,128)(2,1)S(1)} collective-permute-done((bf16[128,1024]{1,0:T(8,128)(2,1)S(1)}, bf16[128,1024]{1,0:T(8,128)(2,1)S(1)}, u32[]{:S(2)}, u32[]{:S(2)}) %collective-permute-start.29) | collective-permute-done | bytes 262176 | tf_op jit(solution)/shard_map/ppermute | solution.py:56
  343.3 5.0 %collective-permute-done.33 = bf16[128,1024]{1,0:T(8,128)(2,1)S(1)} collective-permute-done((bf16[128,1024]{1,0:T(8,128)(2,1)S(1)}, bf16[128,1024]{1,0:T(8,128)(2,1)S(1)}, u32[]{:S(2)}, u32[]{:S(2)}) %collective-permute-start.33) | collective-permute-done | bytes 262176 | tf_op jit(solution)/shard_map/ppermute | solution.py:56
  348.9 5.0 %collective-permute-done.37 = bf16[128,1024]{1,0:T(8,128)(2,1)S(1)} collective-permute-done((bf16[128,1024]{1,0:T(8,128)(2,1)S(1)}, bf16[128,1024]{1,0:T(8,128)(2,1)S(1)}, u32[]{:S(2)}, u32[]{:S(2)}) %collective-permute-start.37) | collective-permute-done | bytes 262176 | tf_op jit(solution)/shard_map/ppermute | solution.py:56
  354.5 1.3 collective-permute-start.30
  356.9 2.6 collective-permute-done.12
  360.9 4.2 %collective-permute-done.18 = bf16[128,1024]{1,0:T(8,128)(2,1)S(1)} collective-permute-done((bf16[128,1024]{1,0:T(8,128)(2,1)S(1)}, bf16[128,1024]{1,0:T(8,128)(2,1)S(1)}, u32[]{:S(2)}, u32[]{:S(2)}) %collective-permute-start.18) | collective-permute-done | bytes 262176 | tf_op jit(solution)/shard_map/ppermute | solution.py:56
  366.5 4.2 %collective-permute-done.22 = bf16[128,1024]{1,0:T(8,128)(2,1)S(1)} collective-permute-done((bf16[128,1024]{1,0:T(8,128)(2,1)S(1)}, bf16[128,1024]{1,0:T(8,128)(2,1)S(1)}, u32[]{:S(2)}, u32[]{:S(2)}) %collective-permute-start.22) | collective-permute-done | bytes 262176 | tf_op jit(solution)/shard_map/ppermute | solution.py:56
  371.6 4.8 %collective-permute-done.26 = bf16[128,1024]{1,0:T(8,128)(2,1)S(1)} collective-permute-done((bf16[128,1024]{1,0:T(8,128)(2,1)S(1)}, bf16[128,1024]{1,0:T(8,128)(2,1)S(1)}, u32[]{:S(2)}, u32[]{:S(2)}) %collective-permute-start.26) | collective-permute-done | bytes 262176 | tf_op jit(solution)/shard_map/ppermute | solution.py:56
  377.2 4.8 %collective-permute-done.30 = bf16[128,1024]{1,0:T(8,128)(2,1)S(1)} collective-permute-done((bf16[128,1024]{1,0:T(8,128)(2,1)S(1)}, bf16[128,1024]{1,0:T(8,128)(2,1)S(1)}, u32[]{:S(2)}, u32[]{:S(2)}) %collective-permute-start.30) | collective-permute-done | bytes 262176 | tf_op jit(solution)/shard_map/ppermute | solution.py:56
  382.8 4.8 %collective-permute-done.34 = bf16[128,1024]{1,0:T(8,128)(2,1)S(1)} collective-permute-done((bf16[128,1024]{1,0:T(8,128)(2,1)S(1)}, bf16[128,1024]{1,0:T(8,128)(2,1)S(1)}, u32[]{:S(2)}, u32[]{:S(2)}) %collective-permute-start.34) | collective-permute-done | bytes 262176 | tf_op jit(solution)/shard_map/ppermute | solution.py:56
  388.4 3.2 collective-permute-done.38
  (195 shorter events, 56.5 us)
Async XLA Ops:
  0.6 14.1 %copy-start = (bf16[128,8192]{1,0:T(8,128)(2,1)S(1)}, bf16[128,8192]{1,0:T(8,128)(2,1)}, u32[]{:S(2)}) copy-start(bf16[128,8192]{1,0:T(8,128)(2,1)} %param.18) | copy-start | bytes 6291460
  15.1 3.9 copy-start.4
  15.1 7.4 %copy-start.14 = (s32[8]{0:T(128)S(1)}, s32[8]{0:T(128)}, u32[]{:S(2)}) copy-start(s32[8]{0:T(128)} %constant.101.clone) | copy-start | bytes 100
  15.1 10.3 %copy-start.13 = (s32[8]{0:T(128)S(1)}, s32[8]{0:T(128)}, u32[]{:S(2)}) copy-start(s32[8]{0:T(128)} %constant.102.clone) | copy-start | bytes 100
  15.1 14.3 %copy-start.12 = (s32[8]{0:T(128)S(1)}, s32[8]{0:T(128)}, u32[]{:S(2)}) copy-start(s32[8]{0:T(128)} %constant.103.clone) | copy-start | bytes 100
  15.1 18.1 %copy-start.11 = (s32[8]{0:T(128)S(1)}, s32[8]{0:T(128)}, u32[]{:S(2)}) copy-start(s32[8]{0:T(128)} %constant.104.clone) | copy-start | bytes 100
  18.9 16.4 %copy-start.10 = (s32[8]{0:T(128)S(1)}, s32[8]{0:T(128)}, u32[]{:S(2)}) copy-start(s32[8]{0:T(128)} %constant.105.clone) | copy-start | bytes 100
  18.9 17.7 %copy-start.9 = (s32[8]{0:T(128)S(1)}, s32[8]{0:T(128)}, u32[]{:S(2)}) copy-start(s32[8]{0:T(128)} %constant.106.clone) | copy-start | bytes 100
  18.9 18.9 %copy-start.8 = (s32[8]{0:T(128)S(1)}, s32[8]{0:T(128)}, u32[]{:S(2)}) copy-start(s32[8]{0:T(128)} %constant.107.clone) | copy-start | bytes 100
  19.0 21.8 %copy-start.5 = (s32[4]{0:T(128)S(1)}, s32[4]{0:T(128)}, u32[]{:S(2)}) copy-start(s32[4]{0:T(128)} %constant.108.clone) | copy-start | bytes 52
  19.4 21.0 %collective-permute-start.13 = (f32[128,32]{0,1:T(8,128)S(1)}, f32[128,32]{0,1:T(8,128)S(1)}, u32[]{:S(2)}, u32[]{:S(2)}) collective-permute-start(f32[128,32]{0,1:T(8,128)S(1)} %pad_maximum_fusion.3), channel_id=1, source_target_pairs={{0,2},{1,3},{2,0},{3,1},{4,6},{5,7},{6,4},{7,5},{8,10},{9,11},{10,... | collective-permute-start | bytes 49160 | tf_op jit(solution)/shard_map/ppermute | solution.py:65
  23.8 39.8 %collective-permute-start = (bf16[128,256]{1,0:T(8,128)(2,1)S(1)}, bf16[128,256]{1,0:T(8,128)(2,1)S(1)}, u32[]{:S(2)}, u32[]{:S(2)}) collective-permute-start(bf16[128,256]{1,0:T(8,128)(2,1)S(1)} %convolution_convert_fusion.26), channel_id=1, source_target_pairs={{4,0},{0,4},{12,8},{8,12},{28,24},{24,28},{20,16},{16,20},{5,1},{1... | collective-permute-start | bytes 196616 | tf_op jit(solution)/shard_map/ppermute | solution.py:138
  26.8 37.0 %collective-permute-start.1 = (bf16[128,256]{1,0:T(8,128)(2,1)S(1)}, bf16[128,256]{1,0:T(8,128)(2,1)S(1)}, u32[]{:S(2)}, u32[]{:S(2)}) collective-permute-start(bf16[128,256]{1,0:T(8,128)(2,1)S(1)} %convolution_convert_fusion.25), channel_id=1, source_target_pairs={{12,0},{8,4},{28,8},{24,12},{20,24},{16,28},{4,16},{0,20},{13,1},{... | collective-permute-start | bytes 196616 | tf_op jit(solution)/shard_map/ppermute | solution.py:138
  30.8 35.4 %collective-permute-start.2 = (bf16[128,256]{1,0:T(8,128)(2,1)S(1)}, bf16[128,256]{1,0:T(8,128)(2,1)S(1)}, u32[]{:S(2)}, u32[]{:S(2)}) collective-permute-start(bf16[128,256]{1,0:T(8,128)(2,1)S(1)} %convolution_convert_fusion.24), channel_id=1, source_target_pairs={{28,0},{24,4},{20,8},{16,12},{4,24},{0,28},{12,16},{8,20},{29,1},{... | collective-permute-start | bytes 196616 | tf_op jit(solution)/shard_map/ppermute | solution.py:138
  34.6 40.6 %collective-permute-start.3 = (bf16[128,256]{1,0:T(8,128)(2,1)S(1)}, bf16[128,256]{1,0:T(8,128)(2,1)S(1)}, u32[]{:S(2)}, u32[]{:S(2)}) collective-permute-start(bf16[128,256]{1,0:T(8,128)(2,1)S(1)} %convolution_convert_fusion.23), channel_id=1, source_target_pairs={{20,0},{16,4},{4,8},{0,12},{12,24},{8,28},{28,16},{24,20},{21,1},{... | collective-permute-start | bytes 196616 | tf_op jit(solution)/shard_map/ppermute | solution.py:138
  40.5 8.7 %collective-permute-start.14 = (f32[128,32]{0,1:T(8,128)S(1)}, f32[128,32]{0,1:T(8,128)S(1)}, u32[]{:S(2)}, u32[]{:S(2)}) collective-permute-start(f32[128,32]{0,1:T(8,128)S(1)} %fusion.230), channel_id=1, source_target_pairs={{0,1},{1,0},{2,3},{3,2},{4,5},{5,4},{6,7},{7,6},{8,9},{9,8},{10,11... | collective-permute-start | bytes 49160 | tf_op jit(solution)/shard_map/ppermute | solution.py:65
  49.2 53.5 %collective-permute-start.4 = (bf16[128,256]{1,0:T(8,128)(2,1)S(1)}, bf16[128,256]{1,0:T(8,128)(2,1)S(1)}, u32[]{:S(2)}, u32[]{:S(2)}) collective-permute-start(bf16[128,256]{1,0:T(8,128)(2,1)S(1)} %convolution_convert_fusion.21), channel_id=1, source_target_pairs={{8,0},{12,4},{24,8},{28,12},{16,24},{20,28},{0,16},{4,20},{9,1},{1... | collective-permute-start | bytes 196616 | tf_op jit(solution)/shard_map/ppermute | solution.py:138
  61.8 57.4 %slice-start = ((s8[14680064]{0:T(1024)(128)(4,1)}), s8[2097152]{0:T(1024)(128)(4,1)S(1)}, s32[]{:S(2)}) async-start(s8[14680064]{0:T(1024)(128)(4,1)} %bitcast.118), calls=%async_computation | async-start | bytes 4194304
  62.1 57.1 %slice-start.1 = ((s8[14680064]{0:T(1024)(128)(4,1)}), s8[4194304]{0:T(1024)(128)(4,1)S(1)}, s32[]{:S(2)}) async-start(s8[14680064]{0:T(1024)(128)(4,1)} %bitcast.118), calls=%async_computation.1 | async-start | bytes 8388608
  63.6 11.5 %collective-permute-start.43 = (bf16[2,32,2048]{2,1,0:T(8,128)(2,1)S(1)}, bf16[2,32,2048]{2,1,0:T(8,128)(2,1)S(1)}, u32[]{:S(2)}, u32[]{:S(2)}) collective-permute-start(bf16[2,32,2048]{2,1,0:T(8,128)(2,1)S(1)} %bitcast.117), channel_id=1, source_target_pairs={{0,8},{4,12},{8,24},{12,28},{24,16},{28,20},{16,0},{20,4},{1,9},{5... | collective-permute-start | bytes 786440 | tf_op jit(solution)/shard_map/ppermute | solution.py:56
  63.8 38.8 %collective-permute-start.5 = (bf16[128,256]{1,0:T(8,128)(2,1)S(1)}, bf16[128,256]{1,0:T(8,128)(2,1)S(1)}, u32[]{:S(2)}, u32[]{:S(2)}) collective-permute-start(bf16[128,256]{1,0:T(8,128)(2,1)S(1)} %convolution_convert_fusion.20), channel_id=1, source_target_pairs={{24,0},{28,4},{16,8},{20,12},{0,24},{4,28},{8,16},{12,20},{25,1},{... | collective-permute-start | bytes 196616 | tf_op jit(solution)/shard_map/ppermute | solution.py:138
  66.2 36.4 %collective-permute-start.6 = (bf16[128,256]{1,0:T(8,128)(2,1)S(1)}, bf16[128,256]{1,0:T(8,128)(2,1)S(1)}, u32[]{:S(2)}, u32[]{:S(2)}) collective-permute-start(bf16[128,256]{1,0:T(8,128)(2,1)S(1)} %convolution_convert_fusion.19), channel_id=1, source_target_pairs={{16,0},{20,4},{0,8},{4,12},{8,24},{12,28},{24,16},{28,20},{17,1},{... | collective-permute-start | bytes 196616 | tf_op jit(solution)/shard_map/ppermute | solution.py:138
  75.1 40.6 %collective-permute-start.39 = (bf16[2,32,7168]{2,1,0:T(8,128)(2,1)S(1)}, bf16[2,32,7168]{2,1,0:T(8,128)(2,1)S(1)}, u32[]{:S(2)}, u32[]{:S(2)}) collective-permute-start(bf16[2,32,7168]{2,1,0:T(8,128)(2,1)S(1)} %bitcast.112), channel_id=1, source_target_pairs={{0,8},{4,12},{8,24},{12,28},{24,16},{28,20},{16,0},{20,4},{1,9},{5... | collective-permute-start | bytes 2752520 | tf_op jit(solution)/shard_map/ppermute | solution.py:56
  75.2 27.3 %collective-permute-start.44 = (bf16[2,32,2048]{2,1,0:T(8,128)(2,1)S(1)}, bf16[2,32,2048]{2,1,0:T(8,128)(2,1)S(1)}, u32[]{:S(2)}, u32[]{:S(2)}) collective-permute-start(bf16[2,32,2048]{2,1,0:T(8,128)(2,1)S(1)} %fusion.121), channel_id=1, source_target_pairs={{0,8},{4,12},{8,24},{12,28},{24,16},{28,20},{16,0},{20,4},{1,9},{5... | collective-permute-start | bytes 786440 | tf_op jit(solution)/shard_map/ppermute | solution.py:56
  102.5 7.3 %collective-permute-start.45 = (bf16[2,32,2048]{2,1,0:T(8,128)(2,1)S(1)}, bf16[2,32,2048]{2,1,0:T(8,128)(2,1)S(1)}, u32[]{:S(2)}, u32[]{:S(2)}) collective-permute-start(bf16[2,32,2048]{2,1,0:T(8,128)(2,1)S(1)} %fusion.122), channel_id=1, source_target_pairs={{0,8},{4,12},{8,24},{12,28},{24,16},{28,20},{16,0},{20,4},{1,9},{5... | collective-permute-start | bytes 786440 | tf_op jit(solution)/shard_map/ppermute | solution.py:56
  102.7 11.6 %collective-permute-start.7 = (bf16[1,1024,256]{2,1,0:T(8,128)(2,1)S(1)}, bf16[1,1024,256]{2,1,0:T(8,128)(2,1)S(1)}, u32[]{:S(2)}, u32[]{:S(2)}) collective-permute-start(bf16[1,1024,256]{2,1,0:T(8,128)(2,1)S(1)} %bitcast.106), channel_id=1, source_target_pairs={{0,2},{1,3},{2,0},{3,1},{4,6},{5,7},{6,4},{7,5},{8,10},{9,11},{10,... | collective-permute-start | bytes 1572872 | tf_op jit(solution)/shard_map/ppermute | solution.py:75
  110.0 5.0 %collective-permute-start.46 = (bf16[32,2048]{1,0:T(8,128)(2,1)S(1)}, bf16[32,2048]{1,0:T(8,128)(2,1)S(1)}, u32[]{:S(2)}, u32[]{:S(2)}) collective-permute-start(bf16[32,2048]{1,0:T(8,128)(2,1)S(1)} %fusion.163), channel_id=1, source_target_pairs={{0,4},{4,0},{8,12},{12,8},{16,20},{20,16},{24,28},{28,24},{1,5},{5... | collective-permute-start | bytes 393224 | tf_op jit(solution)/shard_map/ppermute | solution.py:195
  114.4 4.2 %collective-permute-start.8 = (bf16[2,1024,256]{2,1,0:T(8,128)(2,1)S(1)}, bf16[2,1024,256]{2,1,0:T(8,128)(2,1)S(1)}, u32[]{:S(2)}, u32[]{:S(2)}) collective-permute-start(bf16[2,1024,256]{2,1,0:T(8,128)(2,1)S(1)} %pad_maximum_fusion.2), channel_id=1, source_target_pairs={{0,1},{1,0},{2,3},{3,2},{4,5},{5,4},{6,7},{7,6},{8,9},{9,8},{10,11... | collective-permute-start | bytes 3145736 | tf_op jit(solution)/shard_map/ppermute | solution.py:75
  115.7 3.5 slice-start.2
  115.9 23.3 %collective-permute-start.40 = (bf16[2,32,7168]{2,1,0:T(8,128)(2,1)S(1)}, bf16[2,32,7168]{2,1,0:T(8,128)(2,1)S(1)}, u32[]{:S(2)}, u32[]{:S(2)}) collective-permute-start(bf16[2,32,7168]{2,1,0:T(8,128)(2,1)S(1)} %fusion.30), channel_id=1, source_target_pairs={{0,8},{4,12},{8,24},{12,28},{24,16},{28,20},{16,0},{20,4},{1,9},{5... | collective-permute-start | bytes 2752520 | tf_op jit(solution)/shard_map/ppermute | solution.py:56
  118.7 2.2 slice-start.3
  127.4 26.1 %collective-permute-start.9 = (bf16[512,1024]{1,0:T(8,128)(2,1)S(1)}, bf16[512,1024]{1,0:T(8,128)(2,1)S(1)}, u32[]{:S(2)}, u32[]{:S(2)}) collective-permute-start(bf16[512,1024]{1,0:T(8,128)(2,1)S(1)} %fusion.34), channel_id=1, source_target_pairs={{0,4},{4,0},{8,12},{12,8},{16,20},{20,16},{24,28},{28,24},{1,5},{5... | collective-permute-start | bytes 3145736 | tf_op jit(solution)/shard_map/ppermute | solution.py:209
  129.0 46.9 %collective-permute-start.15 = (bf16[512,1024]{1,0:T(8,128)(2,1)S(1)}, bf16[512,1024]{1,0:T(8,128)(2,1)S(1)}, u32[]{:S(2)}, u32[]{:S(2)}) collective-permute-start(bf16[512,1024]{1,0:T(8,128)(2,1)S(1)} %fusion.37), channel_id=1, source_target_pairs={{0,4},{4,0},{8,12},{12,8},{16,20},{20,16},{24,28},{28,24},{1,5},{5... | collective-permute-start | bytes 3145736 | tf_op jit(solution)/shard_map/ppermute | solution.py:209
  129.5 68.9 %collective-permute-start.19 = (bf16[512,1024]{1,0:T(8,128)(2,1)S(1)}, bf16[512,1024]{1,0:T(8,128)(2,1)S(1)}, u32[]{:S(2)}, u32[]{:S(2)}) collective-permute-start(bf16[512,1024]{1,0:T(8,128)(2,1)S(1)} %fusion.40), channel_id=1, source_target_pairs={{0,4},{4,0},{8,12},{12,8},{16,20},{20,16},{24,28},{28,24},{1,5},{5... | collective-permute-start | bytes 3145736 | tf_op jit(solution)/shard_map/ppermute | solution.py:209
  131.0 89.8 %collective-permute-start.23 = (bf16[512,1024]{1,0:T(8,128)(2,1)S(1)}, bf16[512,1024]{1,0:T(8,128)(2,1)S(1)}, u32[]{:S(2)}, u32[]{:S(2)}) collective-permute-start(bf16[512,1024]{1,0:T(8,128)(2,1)S(1)} %fusion.43), channel_id=1, source_target_pairs={{0,4},{4,0},{8,12},{12,8},{16,20},{20,16},{24,28},{28,24},{1,5},{5... | collective-permute-start | bytes 3145736 | tf_op jit(solution)/shard_map/ppermute | solution.py:209
  139.3 104.0 %collective-permute-start.27 = (bf16[512,1024]{1,0:T(8,128)(2,1)S(1)}, bf16[512,1024]{1,0:T(8,128)(2,1)S(1)}, u32[]{:S(2)}, u32[]{:S(2)}) collective-permute-start(bf16[512,1024]{1,0:T(8,128)(2,1)S(1)} %fusion.46), channel_id=1, source_target_pairs={{0,4},{4,0},{8,12},{12,8},{16,20},{20,16},{24,28},{28,24},{1,5},{5... | collective-permute-start | bytes 3145736 | tf_op jit(solution)/shard_map/ppermute | solution.py:209
  153.4 112.4 %collective-permute-start.31 = (bf16[512,1024]{1,0:T(8,128)(2,1)S(1)}, bf16[512,1024]{1,0:T(8,128)(2,1)S(1)}, u32[]{:S(2)}, u32[]{:S(2)}) collective-permute-start(bf16[512,1024]{1,0:T(8,128)(2,1)S(1)} %fusion.49), channel_id=1, source_target_pairs={{0,4},{4,0},{8,12},{12,8},{16,20},{20,16},{24,28},{28,24},{1,5},{5... | collective-permute-start | bytes 3145736 | tf_op jit(solution)/shard_map/ppermute | solution.py:209
  175.9 111.7 %collective-permute-start.35 = (bf16[512,1024]{1,0:T(8,128)(2,1)S(1)}, bf16[512,1024]{1,0:T(8,128)(2,1)S(1)}, u32[]{:S(2)}, u32[]{:S(2)}) collective-permute-start(bf16[512,1024]{1,0:T(8,128)(2,1)S(1)} %fusion.52), channel_id=1, source_target_pairs={{0,4},{4,0},{8,12},{12,8},{16,20},{20,16},{24,28},{28,24},{1,5},{5... | collective-permute-start | bytes 3145736 | tf_op jit(solution)/shard_map/ppermute | solution.py:209
  198.4 92.0 %collective-permute-start.41 = (bf16[2,32,7168]{2,1,0:T(8,128)(2,1)S(1)}, bf16[2,32,7168]{2,1,0:T(8,128)(2,1)S(1)}, u32[]{:S(2)}, u32[]{:S(2)}) collective-permute-start(bf16[2,32,7168]{2,1,0:T(8,128)(2,1)S(1)} %fusion.31), channel_id=1, source_target_pairs={{0,8},{4,12},{8,24},{12,28},{24,16},{28,20},{16,0},{20,4},{1,9},{5... | collective-permute-start | bytes 2752520 | tf_op jit(solution)/shard_map/ppermute | solution.py:56
  220.9 70.2 %collective-permute-start.10 = (bf16[128,1024]{1,0:T(8,128)(2,1)S(1)}, bf16[128,1024]{1,0:T(8,128)(2,1)S(1)}, u32[]{:S(2)}, u32[]{:S(2)}) collective-permute-start(bf16[128,1024]{1,0:T(8,128)(2,1)S(1)} %slice.303), channel_id=1, source_target_pairs={{0,8},{4,12},{8,24},{12,28},{24,16},{28,20},{16,0},{20,4},{1,9},{5... | collective-permute-start | bytes 786440 | tf_op jit(solution)/shard_map/ppermute | solution.py:56
  243.3 49.2 %collective-permute-start.16 = (bf16[128,1024]{1,0:T(8,128)(2,1)S(1)}, bf16[128,1024]{1,0:T(8,128)(2,1)S(1)}, u32[]{:S(2)}, u32[]{:S(2)}) collective-permute-start(bf16[128,1024]{1,0:T(8,128)(2,1)S(1)} %slice.311), channel_id=1, source_target_pairs={{0,8},{4,12},{8,24},{12,28},{24,16},{28,20},{16,0},{20,4},{1,9},{5... | collective-permute-start | bytes 786440 | tf_op jit(solution)/shard_map/ppermute | solution.py:56
  265.8 28.6 %collective-permute-start.20 = (bf16[128,1024]{1,0:T(8,128)(2,1)S(1)}, bf16[128,1024]{1,0:T(8,128)(2,1)S(1)}, u32[]{:S(2)}, u32[]{:S(2)}) collective-permute-start(bf16[128,1024]{1,0:T(8,128)(2,1)S(1)} %slice.318), channel_id=1, source_target_pairs={{0,8},{4,12},{8,24},{12,28},{24,16},{28,20},{16,0},{20,4},{1,9},{5... | collective-permute-start | bytes 786440 | tf_op jit(solution)/shard_map/ppermute | solution.py:56
  287.6 10.1 %collective-permute-start.24 = (bf16[128,1024]{1,0:T(8,128)(2,1)S(1)}, bf16[128,1024]{1,0:T(8,128)(2,1)S(1)}, u32[]{:S(2)}, u32[]{:S(2)}) collective-permute-start(bf16[128,1024]{1,0:T(8,128)(2,1)S(1)} %slice.325), channel_id=1, source_target_pairs={{0,8},{4,12},{8,24},{12,28},{24,16},{28,20},{16,0},{20,4},{1,9},{5... | collective-permute-start | bytes 786440 | tf_op jit(solution)/shard_map/ppermute | solution.py:56
  290.4 13.0 %collective-permute-start.28 = (bf16[128,1024]{1,0:T(8,128)(2,1)S(1)}, bf16[128,1024]{1,0:T(8,128)(2,1)S(1)}, u32[]{:S(2)}, u32[]{:S(2)}) collective-permute-start(bf16[128,1024]{1,0:T(8,128)(2,1)S(1)} %slice.332), channel_id=1, source_target_pairs={{0,8},{4,12},{8,24},{12,28},{24,16},{28,20},{16,0},{20,4},{1,9},{5... | collective-permute-start | bytes 786440 | tf_op jit(solution)/shard_map/ppermute | solution.py:56
  291.0 17.9 %collective-permute-start.32 = (bf16[128,1024]{1,0:T(8,128)(2,1)S(1)}, bf16[128,1024]{1,0:T(8,128)(2,1)S(1)}, u32[]{:S(2)}, u32[]{:S(2)}) collective-permute-start(bf16[128,1024]{1,0:T(8,128)(2,1)S(1)} %slice.339), channel_id=1, source_target_pairs={{0,8},{4,12},{8,24},{12,28},{24,16},{28,20},{16,0},{20,4},{1,9},{5... | collective-permute-start | bytes 786440 | tf_op jit(solution)/shard_map/ppermute | solution.py:56
  292.6 22.0 %collective-permute-start.36 = (bf16[128,1024]{1,0:T(8,128)(2,1)S(1)}, bf16[128,1024]{1,0:T(8,128)(2,1)S(1)}, u32[]{:S(2)}, u32[]{:S(2)}) collective-permute-start(bf16[128,1024]{1,0:T(8,128)(2,1)S(1)} %slice.346), channel_id=1, source_target_pairs={{0,8},{4,12},{8,24},{12,28},{24,16},{28,20},{16,0},{20,4},{1,9},{5... | collective-permute-start | bytes 786440 | tf_op jit(solution)/shard_map/ppermute | solution.py:56
  294.4 60.1 %collective-permute-start.42 = (bf16[32,7168]{1,0:T(8,128)(2,1)S(1)}, bf16[32,7168]{1,0:T(8,128)(2,1)S(1)}, u32[]{:S(2)}, u32[]{:S(2)}) collective-permute-start(bf16[32,7168]{1,0:T(8,128)(2,1)S(1)} %fusion.125), channel_id=1, source_target_pairs={{0,4},{4,0},{8,12},{12,8},{16,20},{20,16},{24,28},{28,24},{1,5},{5... | collective-permute-start | bytes 1376264 | tf_op jit(solution)/shard_map/ppermute | solution.py:195
  297.7 22.5 %collective-permute-start.11 = (bf16[128,1024]{1,0:T(8,128)(2,1)S(1)}, bf16[128,1024]{1,0:T(8,128)(2,1)S(1)}, u32[]{:S(2)}, u32[]{:S(2)}) collective-permute-start(bf16[128,1024]{1,0:T(8,128)(2,1)S(1)} %add_convert_fusion.20), channel_id=1, source_target_pairs={{0,8},{4,12},{8,24},{12,28},{24,16},{28,20},{16,0},{20,4},{1,9},{5... | collective-permute-start | bytes 786440 | tf_op jit(solution)/shard_map/ppermute | solution.py:56
  303.3 22.5 %collective-permute-start.17 = (bf16[128,1024]{1,0:T(8,128)(2,1)S(1)}, bf16[128,1024]{1,0:T(8,128)(2,1)S(1)}, u32[]{:S(2)}, u32[]{:S(2)}) collective-permute-start(bf16[128,1024]{1,0:T(8,128)(2,1)S(1)} %add_convert_fusion.18), channel_id=1, source_target_pairs={{0,8},{4,12},{8,24},{12,28},{24,16},{28,20},{16,0},{20,4},{1,9},{5... | collective-permute-start | bytes 786440 | tf_op jit(solution)/shard_map/ppermute | solution.py:56
  308.9 22.5 %collective-permute-start.21 = (bf16[128,1024]{1,0:T(8,128)(2,1)S(1)}, bf16[128,1024]{1,0:T(8,128)(2,1)S(1)}, u32[]{:S(2)}, u32[]{:S(2)}) collective-permute-start(bf16[128,1024]{1,0:T(8,128)(2,1)S(1)} %add_convert_fusion.16), channel_id=1, source_target_pairs={{0,8},{4,12},{8,24},{12,28},{24,16},{28,20},{16,0},{20,4},{1,9},{5... | collective-permute-start | bytes 786440 | tf_op jit(solution)/shard_map/ppermute | solution.py:56
  314.6 22.5 %collective-permute-start.25 = (bf16[128,1024]{1,0:T(8,128)(2,1)S(1)}, bf16[128,1024]{1,0:T(8,128)(2,1)S(1)}, u32[]{:S(2)}, u32[]{:S(2)}) collective-permute-start(bf16[128,1024]{1,0:T(8,128)(2,1)S(1)} %add_convert_fusion.14), channel_id=1, source_target_pairs={{0,8},{4,12},{8,24},{12,28},{24,16},{28,20},{16,0},{20,4},{1,9},{5... | collective-permute-start | bytes 786440 | tf_op jit(solution)/shard_map/ppermute | solution.py:56
  315.1 44.9 %copy-start.15 = (f32[128,7168]{1,0:T(8,128)S(1)}, f32[128,7168]{1,0:T(8,128)}, u32[]{:S(2)}) copy-start(f32[128,7168]{1,0:T(8,128)} %get-tuple-element.26) | copy-start | bytes 11010052
  320.2 22.5 %collective-permute-start.29 = (bf16[128,1024]{1,0:T(8,128)(2,1)S(1)}, bf16[128,1024]{1,0:T(8,128)(2,1)S(1)}, u32[]{:S(2)}, u32[]{:S(2)}) collective-permute-start(bf16[128,1024]{1,0:T(8,128)(2,1)S(1)} %add_convert_fusion.12), channel_id=1, source_target_pairs={{0,8},{4,12},{8,24},{12,28},{24,16},{28,20},{16,0},{20,4},{1,9},{5... | collective-permute-start | bytes 786440 | tf_op jit(solution)/shard_map/ppermute | solution.py:56
  325.8 22.5 %collective-permute-start.33 = (bf16[128,1024]{1,0:T(8,128)(2,1)S(1)}, bf16[128,1024]{1,0:T(8,128)(2,1)S(1)}, u32[]{:S(2)}, u32[]{:S(2)}) collective-permute-start(bf16[128,1024]{1,0:T(8,128)(2,1)S(1)} %add_convert_fusion.10), channel_id=1, source_target_pairs={{0,8},{4,12},{8,24},{12,28},{24,16},{28,20},{16,0},{20,4},{1,9},{5... | collective-permute-start | bytes 786440 | tf_op jit(solution)/shard_map/ppermute | solution.py:56
  331.4 22.5 %collective-permute-start.37 = (bf16[128,1024]{1,0:T(8,128)(2,1)S(1)}, bf16[128,1024]{1,0:T(8,128)(2,1)S(1)}, u32[]{:S(2)}, u32[]{:S(2)}) collective-permute-start(bf16[128,1024]{1,0:T(8,128)(2,1)S(1)} %add_convert_fusion.8), channel_id=1, source_target_pairs={{0,8},{4,12},{8,24},{12,28},{24,16},{28,20},{16,0},{20,4},{1,9},{5... | collective-permute-start | bytes 786440 | tf_op jit(solution)/shard_map/ppermute | solution.py:56
  337.0 22.5 %collective-permute-start.12 = (bf16[128,1024]{1,0:T(8,128)(2,1)S(1)}, bf16[128,1024]{1,0:T(8,128)(2,1)S(1)}, u32[]{:S(2)}, u32[]{:S(2)}) collective-permute-start(bf16[128,1024]{1,0:T(8,128)(2,1)S(1)} %add_convert_fusion.19), channel_id=1, source_target_pairs={{0,8},{4,12},{8,24},{12,28},{24,16},{28,20},{16,0},{20,4},{1,9},{5... | collective-permute-start | bytes 786440 | tf_op jit(solution)/shard_map/ppermute | solution.py:56
  342.6 22.5 %collective-permute-start.18 = (bf16[128,1024]{1,0:T(8,128)(2,1)S(1)}, bf16[128,1024]{1,0:T(8,128)(2,1)S(1)}, u32[]{:S(2)}, u32[]{:S(2)}) collective-permute-start(bf16[128,1024]{1,0:T(8,128)(2,1)S(1)} %add_convert_fusion.17), channel_id=1, source_target_pairs={{0,8},{4,12},{8,24},{12,28},{24,16},{28,20},{16,0},{20,4},{1,9},{5... | collective-permute-start | bytes 786440 | tf_op jit(solution)/shard_map/ppermute | solution.py:56
  343.3 16.8 %copy-start.2 = (f32[128,7168]{1,0:T(8,128)S(1)}, f32[128,7168]{1,0:T(8,128)}, u32[]{:S(2)}) copy-start(f32[128,7168]{1,0:T(8,128)} %fusion.1) | copy-start | bytes 11010052
  348.3 22.5 %collective-permute-start.22 = (bf16[128,1024]{1,0:T(8,128)(2,1)S(1)}, bf16[128,1024]{1,0:T(8,128)(2,1)S(1)}, u32[]{:S(2)}, u32[]{:S(2)}) collective-permute-start(bf16[128,1024]{1,0:T(8,128)(2,1)S(1)} %add_convert_fusion.15), channel_id=1, source_target_pairs={{0,8},{4,12},{8,24},{12,28},{24,16},{28,20},{16,0},{20,4},{1,9},{5... | collective-permute-start | bytes 786440 | tf_op jit(solution)/shard_map/ppermute | solution.py:56
  353.9 22.5 %collective-permute-start.26 = (bf16[128,1024]{1,0:T(8,128)(2,1)S(1)}, bf16[128,1024]{1,0:T(8,128)(2,1)S(1)}, u32[]{:S(2)}, u32[]{:S(2)}) collective-permute-start(bf16[128,1024]{1,0:T(8,128)(2,1)S(1)} %add_convert_fusion.13), channel_id=1, source_target_pairs={{0,8},{4,12},{8,24},{12,28},{24,16},{28,20},{16,0},{20,4},{1,9},{5... | collective-permute-start | bytes 786440 | tf_op jit(solution)/shard_map/ppermute | solution.py:56
  354.5 27.4 %collective-permute-start.30 = (bf16[128,1024]{1,0:T(8,128)(2,1)S(1)}, bf16[128,1024]{1,0:T(8,128)(2,1)S(1)}, u32[]{:S(2)}, u32[]{:S(2)}) collective-permute-start(bf16[128,1024]{1,0:T(8,128)(2,1)S(1)} %add_convert_fusion.11), channel_id=1, source_target_pairs={{0,8},{4,12},{8,24},{12,28},{24,16},{28,20},{16,0},{20,4},{1,9},{5... | collective-permute-start | bytes 786440 | tf_op jit(solution)/shard_map/ppermute | solution.py:56
  359.5 28.1 %collective-permute-start.34 = (bf16[128,1024]{1,0:T(8,128)(2,1)S(1)}, bf16[128,1024]{1,0:T(8,128)(2,1)S(1)}, u32[]{:S(2)}, u32[]{:S(2)}) collective-permute-start(bf16[128,1024]{1,0:T(8,128)(2,1)S(1)} %add_convert_fusion.9), channel_id=1, source_target_pairs={{0,8},{4,12},{8,24},{12,28},{24,16},{28,20},{16,0},{20,4},{1,9},{5... | collective-permute-start | bytes 786440 | tf_op jit(solution)/shard_map/ppermute | solution.py:56
  365.1 26.5 %collective-permute-start.38 = (bf16[128,1024]{1,0:T(8,128)(2,1)S(1)}, bf16[128,1024]{1,0:T(8,128)(2,1)S(1)}, u32[]{:S(2)}, u32[]{:S(2)}) collective-permute-start(bf16[128,1024]{1,0:T(8,128)(2,1)S(1)} %add_convert_fusion.7), channel_id=1, source_target_pairs={{0,8},{4,12},{8,24},{12,28},{24,16},{28,20},{16,0},{20,4},{1,9},{5... | collective-permute-start | bytes 786440 | tf_op jit(solution)/shard_map/ppermute | solution.py:56
  391.6 2.2 copy-start.1
  (3 other events, 4.1 us)
